TPU v7x, 32 devices: a whole 2x2x4 slice. The times are simulated.
32 devices in a mesh: patch: 2 (over y), space: 4 (over z), tm: 2 (over x), row: 2 (over core).
Axes of the slice: x: 2, y: 2, z: 4, core: 2. Of those that a mesh axis runs over, the one named last changes fastest.
Arguments:
- doppler: float32 [32, 192, 256], P('tm', ('patch', 'space'), 'row'), parts along dimension 1, may hold values from -24 to 24
- cycle_masks: int32 [8, 33, 33], replicated, may hold values from 0 to 1, as said below
- lag_list: int32 [4], replicated, may hold values from 1 to 16, as said below
Outputs:
- correlations: float32 [2, 8, 4, 192, 256], P('tm', None, None, ('patch', 'space'), 'row'), parts along dimension 3
There are 2 independent parts, one for each index of `patch`. A program takes and returns all parts, laid end to end along the dimension named above; an argument that names none is the same for every part. Nothing has to cross between parts.
Inputs may be any that keep to these rules, and one draw needn't show every extreme that they name: Each cycle_masks[r] is 1 only at offsets whose distance from the centre lies within half a pixel of one radius of 1 to 16, distinct radii over r, and is 1 at the offsets of that radius along both pixel directions; one annulus has radius 16. `lag_list`: the lags are distinct and one of them is 16.
All inputs are finite; a program needn't handle non-finite values.
Results may differ from a plain program's by a relative error of at most 0.0033.
Values may be sent and summed in bfloat16 or wider, within the bound.
A program may use at most 64 MiB of HBM per device.

v0:
```python
import functools

import jax
import jax.numpy as jnp
from jax import lax
from jax.experimental import pallas as pl
from jax.experimental.pallas import tpu as pltpu
from jax.sharding import PartitionSpec as P

MESH = pl.DeviceIdType.MESH
RMAX = 16
LANES = 128
TILE = 32
SPAN = 2 * TILE
PACK = LANES // TILE
gaussian_taps = (0.05448868, 0.24420134, 0.40261995, 0.24420134, 0.05448868)
REACH = len(gaussian_taps) // 2


def lane_iota(shape):
    return lax.broadcasted_iota(jnp.int32, shape, len(shape) - 1)


def pack_borders(blocks, side):
    group = lane_iota(blocks[0].shape) // TILE
    base = (1 - side) * TILE
    packed = None
    for k, block in enumerate(blocks):
        turned = pltpu.roll(block, lax.rem(k * TILE + base, LANES), 1)
        packed = turned if packed is None else jnp.where(group == k, turned, packed)
    return packed


def unpack_border(packed, k, side):
    base = side * (LANES - TILE)
    turned = pltpu.roll(packed, lax.rem(LANES - k * TILE + base, LANES), 1)
    lane = lane_iota(packed.shape)
    return jnp.where((lane >= base) & (lane < base + TILE), turned, jnp.zeros_like(turned))


def exchange_body(frames, cols, dop, field, halo, series, wide, packs, packed16, halo_in, unpacked,
                  natural, send, recv):
    count_s, count_t = lax.axis_size("space"), lax.axis_size("tm")
    s, t, side = lax.axis_index("space"), lax.axis_index("tm"), lax.axis_index("row")
    has_lo, has_hi = s > 0, s < count_s - 1
    has_pr, has_nx = t > 0, t < count_t - 1
    lo, hi = {"space": s - 1}, {"space": s + 1}
    lo_x, hi_x = {"space": s - 1, "row": 1 - side}, {"space": s + 1, "row": 1 - side}
    partner = {"row": 1 - side}
    prev, nxt = {"tm": t - 1}, {"tm": t + 1}
    groups = cols // PACK
    reach_groups = RMAX // PACK
    top = RMAX + cols
    sent = frames * cols
    always = None

    def when(cond, act):
        if cond is None:
            act()
        else:
            pl.when(cond)(act)

    barrier = pltpu.get_barrier_semaphore()

    def greet(*devices):
        def act():
            for device in devices:
                pl.semaphore_signal(barrier, inc=1, device_id=device, device_id_type=MESH)
        return act

    greet(partner)()
    pl.when(has_lo)(greet(lo, lo_x))
    pl.when(has_hi)(greet(hi, hi_x))
    pl.when(has_pr)(greet(prev))
    pl.when(has_nx)(greet(nxt))

    for c in range(cols):
        wide[REACH + c] = dop[pl.ds(c, frames, stride=cols), :]
    for g in range(groups):
        packs[g] = pack_borders([wide[REACH + g * PACK + k] for k in range(PACK)], side)

    def zero(ref, start, size):
        def act():
            ref[pl.ds(start, size)] = jnp.zeros((size,) + ref.shape[1:], ref.dtype)
        return act

    no_lo, no_hi, no_pr = s == 0, s == count_s - 1, t == 0
    field[pl.ds(top + RMAX, 1)] = jnp.zeros((1, frames, LANES), field.dtype)
    for cond, low in ((no_lo, True), (no_hi, False)):
        pl.when(cond)(zero(wide, 0 if low else REACH + cols, REACH))
        pl.when(cond)(zero(halo_in, 0 if low else groups + 1, 1))
        pl.when(cond)(zero(field, 0 if low else top, RMAX))
        pl.when(cond)(zero(halo, 0 if low else reach_groups + groups, reach_groups))
    pl.when(no_pr)(zero(series, 0, sent))

    def copy(index, source, target, device):
        return pltpu.make_async_remote_copy(
            src_ref=source, dst_ref=target, send_sem=send.at[index], recv_sem=recv.at[index],
            device_id=device, device_id_type=MESH,
        )

    first = [
        (copy(0, wide.at[pl.ds(REACH, REACH)], wide.at[pl.ds(REACH + cols, REACH)], lo), has_lo, has_hi),
        (copy(1, wide.at[pl.ds(cols, REACH)], wide.at[pl.ds(0, REACH)], hi), has_hi, has_lo),
        (copy(2, packs, halo_in.at[pl.ds(1, groups)], partner), always, always),
        (copy(3, packs.at[pl.ds(0, 1)], halo_in.at[pl.ds(groups + 1, 1)], lo_x), has_lo, has_hi),
        (copy(4, packs.at[pl.ds(groups - 1, 1)], halo_in.at[pl.ds(0, 1)], hi_x), has_hi, has_lo),
    ]
    second = [
        (copy(5, field.at[pl.ds(RMAX, RMAX)], field.at[pl.ds(top, RMAX)], lo), has_lo, has_hi),
        (copy(6, field.at[pl.ds(cols, RMAX)], field.at[pl.ds(0, RMAX)], hi), has_hi, has_lo),
        (copy(7, packed16, halo.at[pl.ds(reach_groups, groups)], partner), always, always),
        (copy(8, packed16.at[pl.ds(0, reach_groups)],
              halo.at[pl.ds(reach_groups + groups, reach_groups)], lo_x), has_lo, has_hi),
        (copy(9, packed16.at[pl.ds(groups - reach_groups, reach_groups)],
              halo.at[pl.ds(0, reach_groups)], hi_x), has_hi, has_lo),
        (copy(10, series.at[pl.ds(sent, sent)], series.at[pl.ds(0, sent)], nxt), has_nx, has_pr),
    ]

    met = lambda flag: jnp.where(flag, 1, 0).astype(jnp.int32)
    pl.semaphore_wait(barrier, 1 + 2 * met(has_lo) + 2 * met(has_hi) + met(has_pr) + met(has_nx))
    for moved, sends, _ in first:
        when(sends, moved.start)
    for moved, _, receives in first:
        when(receives, moved.wait_recv)

    for i in range(cols + 2 * REACH):
        place = i + PACK - REACH
        unpacked[i] = unpack_border(halo_in[place // PACK], place % PACK, side)
    lane = lane_iota((frames, LANES))
    for g in range(groups):
        smoothed = []
        for k in range(PACK):
            c = g * PACK + k
            own, other = [
                functools.reduce(lambda a, b: a + b, [gaussian_taps[i] * ref[c + i] for i in range(len(gaussian_taps))])
                for ref in (wide, unpacked)
            ]
            total = None
            for i, tap in enumerate(gaussian_taps):
                shift = i - REACH
                if shift > 0:
                    moved = pltpu.roll(jnp.where(lane < shift, other, own), LANES - shift, 1)
                elif shift < 0:
                    moved = pltpu.roll(jnp.where(lane >= LANES + shift, other, own), -shift, 1)
                else:
                    moved = own
                total = tap * moved if total is None else total + tap * moved
            smoothed.append(total)
            field[RMAX + c] = total.astype(field.dtype)
            natural[pl.ds(c, frames, stride=cols), :] = total
        packed16[g] = pack_borders(smoothed, side).astype(packed16.dtype)
    series[pl.ds(sent, sent)] = natural[...].astype(series.dtype)

    for moved, sends, _ in second:
        when(sends, moved.start)
    for moved, sends, _ in first:
        when(sends, moved.wait_send)
    for moved, _, receives in second:
        when(receives, moved.wait_recv)
    for moved, sends, _ in second:
        when(sends, moved.wait_send)


def build_bands(radii, width, mask, bands):
    for q in range(TILE):
        for block in range(width // LANES):
            piece = mask[:, pl.ds(block * LANES, LANES)]
            bands[block, pl.ds(q, radii, stride=TILE), :] = piece if q == 0 else pltpu.roll(piece, q, 1)


def correlate_body(frames, cols, radii, lags, lag_list, mask, field, halo, series, out, bands, windows,
                   sums, spread, parts):
    side = lax.axis_index("row")
    tiles = LANES // TILE
    width = mask.shape[1]
    pairs = width // LANES
    build_bands(radii, width, mask, bands)

    lane = lane_iota((frames, LANES))
    previous = [None] * tiles
    f32 = jnp.float32
    total_cols = cols + 2 * RMAX
    for i in range(total_cols + 1):
        own = field[i].astype(f32)
        if i < total_cols:
            other = unpack_border(halo[i // PACK].astype(f32), i % PACK, side)
        else:
            other = jnp.zeros_like(own)
        for j in range(tiles):
            source = own
            if j == 0:
                source = jnp.where(lane >= LANES - RMAX, other, own)
            if j == tiles - 1:
                source = jnp.where(lane < RMAX, other, source)
            shift = (RMAX - TILE * j) % LANES
            odd = pltpu.roll(source, (shift + SPAN) % LANES, 1)
            if i > 0:
                windows[j, i - 1] = jnp.where(lane < SPAN, previous[j], odd).astype(jnp.bfloat16)
            if i < total_cols:
                previous[j] = pltpu.roll(source, shift, 1)

    rows = lax.broadcasted_iota(jnp.int32, (LANES, tiles * LANES), 0)
    places = lax.broadcasted_iota(jnp.int32, (LANES, tiles * LANES), 1)
    pick = jnp.where(rows == (places // LANES) * TILE + places % TILE, 1.0, 0.0).astype(jnp.bfloat16)
    spread[...] = jnp.dot(series[...], pick, preferred_element_type=f32)

    weights = jnp.concatenate([bands[g].astype(jnp.bfloat16) for g in range(pairs)], axis=1)
    halves = radii * TILE // LANES
    for j in range(tiles):
        left = jnp.concatenate(
            [windows[j, pl.ds(2 * g, cols)].reshape(cols * frames, LANES) for g in range(pairs)], axis=1
        )
        total = lax.dot_general(left, weights, (((1,), (1,)), ((), ())), preferred_element_type=f32)
        for h in range(halves):
            sums[j, h] = total[:, h * LANES : (h + 1) * LANES]

    starts = [frames - lag_list[l] for l in range(lags)]
    for j in range(tiles):
        totals = [[None] * halves for _ in range(lags)]
        for t in range(frames):
            annulus = [sums[j, h, pl.ds(t, cols, stride=frames), :] for h in range(halves)]
            for l in range(lags):
                begin = pl.multiple_of((starts[l] + t) * cols, 8)
                earlier = spread[pl.ds(begin, cols), pl.ds(j * LANES, LANES)]
                for h in range(halves):
                    term = earlier * annulus[h]
                    totals[l][h] = term if t == 0 else totals[l][h] + term
        for l in range(lags):
            for h in range(halves):
                parts[j, l, h] = totals[l][h]

    counts = jnp.sum(mask[...], axis=1, keepdims=True)
    group = lane_iota((cols, LANES)) // TILE
    for r in range(radii):
        h, rr = r // PACK, r % PACK
        count = counts[r : r + 1, 0:1]
        for l in range(lags):
            whole = None
            for j in range(tiles):
                shift = (TILE * (j - rr)) % LANES
                piece = parts[j, l, h]
                piece = pltpu.roll(piece, shift, 1) if shift else piece
                whole = piece if whole is None else jnp.where(group == j, piece, whole)
            out[r, l] = whole / count


def local(doppler, cycle_masks, lag_list):
    frames, cols, rows = doppler.shape
    radii, side = cycle_masks.shape[:2]
    lags = lag_list.shape[0]
    assert rows == LANES and frames == RMAX and side == 2 * RMAX + 1 and cols % 8 == 0 and cols >= RMAX
    assert lax.axis_size("row") == 2 and radii * TILE % LANES == 0
    mask = jnp.pad(cycle_masks.astype(jnp.float32), ((0, 0), (0, side % 2), (0, SPAN - side)))
    mask = mask.reshape(radii, -1)
    groups = cols // PACK
    ext = cols + 2 * RMAX
    f32, bf16 = jnp.float32, jnp.bfloat16
    vmem = pl.BlockSpec(memory_space=pltpu.VMEM)
    field, halo, series = pl.pallas_call(
        functools.partial(exchange_body, frames, cols),
        out_shape=(
            jax.ShapeDtypeStruct((ext + 1, frames, LANES), bf16),
            jax.ShapeDtypeStruct((ext // PACK, frames, LANES), bf16),
            jax.ShapeDtypeStruct((2 * frames * cols, LANES), bf16),
        ),
        in_specs=[vmem],
        out_specs=(vmem, vmem, vmem),
        scratch_shapes=[
            pltpu.VMEM((cols + 2 * REACH, frames, LANES), f32),
            pltpu.VMEM((groups, frames, LANES), f32),
            pltpu.VMEM((groups, frames, LANES), bf16),
            pltpu.VMEM((groups + 2, frames, LANES), f32),
            pltpu.VMEM((cols + 2 * REACH, frames, LANES), f32),
            pltpu.VMEM((frames * cols, LANES), f32),
            pltpu.SemaphoreType.DMA((11,)),
            pltpu.SemaphoreType.DMA((11,)),
        ],
        compiler_params=pltpu.CompilerParams(
            collective_id=0, has_side_effects=True, vmem_limit_bytes=32 * 2**20
        ),
    )(doppler.reshape(frames * cols, LANES))
    tiles = LANES // TILE
    out = pl.pallas_call(
        functools.partial(correlate_body, frames, cols, radii, lags),
        out_shape=jax.ShapeDtypeStruct((radii, lags, cols, LANES), f32),
        in_specs=[pl.BlockSpec(memory_space=pltpu.SMEM), vmem, vmem, vmem, vmem],
        out_specs=vmem,
        scratch_shapes=[
            pltpu.VMEM((mask.shape[1] // LANES, radii * TILE, LANES), f32),
            pltpu.VMEM((tiles, ext, frames, LANES), bf16),
            pltpu.VMEM((tiles, radii * TILE // LANES, cols * frames, LANES), f32),
            pltpu.VMEM((2 * frames * cols, tiles * LANES), f32),
            pltpu.VMEM((tiles, lags, radii * TILE // LANES, cols, LANES), f32),
        ],
        compiler_params=pltpu.CompilerParams(vmem_limit_bytes=48 * 2**20),
    )(lag_list, mask, field, halo, series)
    return out[None]


def solution(mesh):
    return jax.shard_map(
        local,
        mesh=mesh,
        in_specs=(P("tm", ("patch", "space"), "row"), P(), P()),
        out_specs=P("tm", None, None, ("patch", "space"), "row"),
        check_vma=False,
    )
```

profile of v0, /device:TPU:0, one launch (start us, length us, event | category | flops | bytes accessed | tf_op | source)
XLA Modules:
  0.0 19.6 jit_solution(13689952814496621899)
XLA Ops:
  0.0 0.9 %convert_element_type.5 = f32[8,33,33]{2,0,1:T(8,128)S(1)} convert(s32[8,33,33]{2,0,1:T(8,128)} %param.4) | non-fusion elementwise | flops 8712 | bytes 69696 | tf_op jit(solution)/shard_map/convert_element_type | solution.py:254
  1.0 0.0 copy-start
  1.0 0.1 reshape.6.mask
  1.1 0.8 %copy-done = f32[16,24,128]{2,1,0:T(8,128)S(1)} copy-done((f32[16,24,128]{2,1,0:T(8,128)S(1)}, f32[16,24,128]{2,1,0:T(8,128)}, u32[]{:S(2)}) %copy-start) | copy-done | bytes 196632
  1.9 11.2 %shard_map.37 = (bf16[57,16,128]{2,1,0:T(8,128)(2,1)S(1)}, bf16[14,16,128]{2,1,0:T(8,128)(2,1)S(1)}, bf16[768,128]{1,0:T(8,128)(2,1)S(1)}) custom-call(f32[384,128]{1,0:T(8,128)S(1)} %bitcast.2), custom_call_target="tpu_custom_call" | custom-call | tf_op jit(solution)/shard_map/pallas_call | solution.py:260
  13.1 0.0 copy-start.1
  13.1 0.6 %copy-done.1 = s32[4]{0:T(128)S(1)} copy-done((s32[4]{0:T(128)S(1)}, s32[4]{0:T(128)}, u32[]{:S(2)}) %copy-start.1) | copy-done | bytes 40
  13.8 5.9 %shard_map.38 = f32[8,4,24,128]{3,2,1,0:T(8,128)} custom-call(s32[4]{0:T(128)S(1)} %copy-done.1, f32[8,2176]{1,0:T(8,128)S(1)} %reshape.6.mask, bf16[57,16,128]{2,1,0:T(8,128)(2,1)S(1)} %get-tuple-element.8.field, bf16[14,16,128]{2,1,0:T(8,128)(2,1)S(1)} %get-tuple-element.9.halo, bf16[768,128]{1,0:T(8,128)(2,1)S(1)} %get-tuple-element.10.series), custom_call_target="tpu_custom_call" | custom-call | tf_op jit(solution)/shard_map/pallas_call | solution.py:284
  (2 shorter events, 0.0 us)
Async XLA Ops:
  1.0 0.9 %copy-start = (f32[16,24,128]{2,1,0:T(8,128)S(1)}, f32[16,24,128]{2,1,0:T(8,128)}, u32[]{:S(2)}) copy-start(f32[16,24,128]{2,1,0:T(8,128)} %param.3) | copy-start | bytes 589828
  13.1 0.7 %copy-start.1 = (s32[4]{0:T(128)S(1)}, s32[4]{0:T(128)}, u32[]{:S(2)}) copy-start(s32[4]{0:T(128)} %lag_list.1) | copy-start | bytes 52
where the time goes:
time: 19.8 us; the launch traced here: 19.6 us
  Pallas kernels  17 us (86%)
  local copies, waits for them, and re-layouts  1.62 us (8%)
  other arithmetic  0.92 us (5%)
    pallas_call x1, Pallas kernels, local(): pl.pallas_call(functools.partial(exchange_body, frames, cols), out_shape=...  11.2 us
    pallas_call x1, Pallas kernels, local(): pl.pallas_call(functools.partial(correlate_body, frames, cols, radii, lag...  5.86 us
    unnamed x5, local copies, waits for them, and re-layouts  1.51 us
    convert_element_type x1, other arithmetic, local(): cycle_masks.astype(jnp.float32)  0.92 us

commit v1 on v0

--- a/solution.py
+++ b/solution.py
@@ -15,6 +15,7 @@
 PACK = LANES // TILE
 gaussian_taps = (0.05448868, 0.24420134, 0.40261995, 0.24420134, 0.05448868)
 REACH = len(gaussian_taps) // 2
+VMEM_SHARE = 24 * 2**20
 
 
 def lane_iota(shape):
@@ -38,8 +39,60 @@
     return jnp.where((lane >= base) & (lane < base + TILE), turned, jnp.zeros_like(turned))
 
 
-def exchange_body(frames, cols, dop, field, halo, series, wide, packs, packed16, halo_in, unpacked,
-                  natural, send, recv):
+def build_weights(radii, mask_in, bands, weights, counts):
+    side = mask_in.shape[0]
+    pairs = weights.shape[0] // LANES
+    bits = mask_in[...].astype(jnp.float32).reshape(side * radii, side).astype(jnp.bfloat16)
+    rows = lax.broadcasted_iota(jnp.int32, (side, LANES), 0)
+    lane = lane_iota((side, LANES))
+    put = [jnp.where(lane == rows + k * SPAN, 1.0, 0.0).astype(jnp.bfloat16) for k in range(2)]
+    even, odd = [jnp.dot(bits, p, preferred_element_type=jnp.float32) for p in put]
+    total = None
+    for g in range(pairs):
+        a = 2 * g
+        piece = even[a * radii : (a + 1) * radii]
+        if a + 1 < side:
+            piece = piece + odd[(a + 1) * radii : (a + 2) * radii]
+        total = piece if total is None else total + piece
+        for q in range(TILE):
+            bands[g, pl.ds(q, radii, stride=TILE), :] = pltpu.roll(piece, q, 1) if q else piece
+        weights[pl.ds(g * LANES, LANES), :] = bands[g].T.astype(weights.dtype)
+    counts[...] = jnp.broadcast_to(jnp.sum(total, axis=1, keepdims=True), counts.shape)
+
+
+def build_windows(places, frames, total_cols, side, field, halo, windows):
+    lane = lane_iota((frames, LANES))
+    tiles = windows.shape[0]
+    sources = {}
+
+    def source(i, j):
+        if i not in sources:
+            own = field[i].astype(jnp.float32)
+            other = jnp.zeros_like(own)
+            if i < total_cols:
+                other = unpack_border(halo[i // PACK].astype(jnp.float32), i % PACK, side)
+            mixed = [own] * tiles
+            mixed[0] = jnp.where(lane >= LANES - RMAX, other, own)
+            mixed[-1] = jnp.where(lane < RMAX, other, own)
+            sources[i] = mixed
+        return sources[i][j]
+
+    for i in places:
+        for j in range(tiles):
+            shift = (RMAX - TILE * j) % LANES
+            first = pltpu.roll(source(i, j), shift, 1)
+            second = pltpu.roll(source(i + 1, j), (shift + SPAN) % LANES, 1)
+            windows[j, i] = jnp.where(lane < SPAN, first, second).astype(windows.dtype)
+
+
+def annulus_body(frames, cols, radii, dop_far, mask_far, lag_far, sums, counts, series, lag_near, dop, mask_in, bands, weights,
+                 field, halo, windows, wide, packs, packed16, halo_in, unpacked, natural, local_sem, send, recv):
+    fetch_dop = pltpu.make_async_copy(dop_far, dop, local_sem.at[0])
+    fetch_mask = pltpu.make_async_copy(mask_far, mask_in, local_sem.at[1])
+    fetch_dop.start()
+    fetch_mask.start()
+    fetch_lags = pltpu.make_async_copy(lag_far, lag_near, local_sem.at[2])
+    fetch_lags.start()
     count_s, count_t = lax.axis_size("space"), lax.axis_size("tm")
     s, t, side = lax.axis_index("space"), lax.axis_index("tm"), lax.axis_index("row")
     has_lo, has_hi = s > 0, s < count_s - 1
@@ -74,6 +127,7 @@
     pl.when(has_pr)(greet(prev))
     pl.when(has_nx)(greet(nxt))
 
+    fetch_dop.wait()
     for c in range(cols):
         wide[REACH + c] = dop[pl.ds(c, frames, stride=cols), :]
     for g in range(groups):
@@ -121,6 +175,9 @@
     pl.semaphore_wait(barrier, 1 + 2 * met(has_lo) + 2 * met(has_hi) + met(has_pr) + met(has_nx))
     for moved, sends, _ in first:
         when(sends, moved.start)
+    fetch_mask.wait()
+    fetch_lags.wait()
+    build_weights(radii, mask_in, bands, weights, counts)
     for moved, _, receives in first:
         when(receives, moved.wait_recv)
 
@@ -156,65 +213,40 @@
         when(sends, moved.start)
     for moved, sends, _ in first:
         when(sends, moved.wait_send)
-    for moved, _, receives in second:
+    second[2][0].wait_recv()
+    build_windows(range(RMAX, top - 1), frames, top + RMAX, side, field, halo, windows)
+    for moved, _, receives in second[:2] + second[3:5]:
         when(receives, moved.wait_recv)
+    rest = list(range(RMAX)) + list(range(top - 1, top + RMAX))
+    build_windows(rest, frames, top + RMAX, side, field, halo, windows)
+
+    pairs = weights.shape[0] // LANES
+    halves = sums.shape[1]
+    for j in range(sums.shape[0]):
+        left = jnp.concatenate(
+            [windows[j, pl.ds(2 * g, cols)].reshape(cols * frames, LANES) for g in range(pairs)], axis=1
+        )
+        total = jnp.dot(left, weights[...], preferred_element_type=jnp.float32)
+        for h in range(halves):
+            sums[j, h] = total[:, h * LANES : (h + 1) * LANES]
+
+    when(has_pr, second[5][0].wait_recv)
     for moved, sends, _ in second:
         when(sends, moved.wait_send)
 
 
-def build_bands(radii, width, mask, bands):
-    for q in range(TILE):
-        for block in range(width // LANES):
-            piece = mask[:, pl.ds(block * LANES, LANES)]
-            bands[block, pl.ds(q, radii, stride=TILE), :] = piece if q == 0 else pltpu.roll(piece, q, 1)
-
-
-def correlate_body(frames, cols, radii, lags, lag_list, mask, field, halo, series, out, bands, windows,
-                   sums, spread, parts):
-    side = lax.axis_index("row")
+def correlate_body(frames, cols, radii, lags, lag_far, counts, series, sums, out, lag_list, spread, parts, sem):
+    fetch = pltpu.make_async_copy(lag_far, lag_list, sem)
+    fetch.start()
     tiles = LANES // TILE
-    width = mask.shape[1]
-    pairs = width // LANES
-    build_bands(radii, width, mask, bands)
-
-    lane = lane_iota((frames, LANES))
-    previous = [None] * tiles
     f32 = jnp.float32
-    total_cols = cols + 2 * RMAX
-    for i in range(total_cols + 1):
-        own = field[i].astype(f32)
-        if i < total_cols:
-            other = unpack_border(halo[i // PACK].astype(f32), i % PACK, side)
-        else:
-            other = jnp.zeros_like(own)
-        for j in range(tiles):
-            source = own
-            if j == 0:
-                source = jnp.where(lane >= LANES - RMAX, other, own)
-            if j == tiles - 1:
-                source = jnp.where(lane < RMAX, other, source)
-            shift = (RMAX - TILE * j) % LANES
-            odd = pltpu.roll(source, (shift + SPAN) % LANES, 1)
-            if i > 0:
-                windows[j, i - 1] = jnp.where(lane < SPAN, previous[j], odd).astype(jnp.bfloat16)
-            if i < total_cols:
-                previous[j] = pltpu.roll(source, shift, 1)
-
     rows = lax.broadcasted_iota(jnp.int32, (LANES, tiles * LANES), 0)
     places = lax.broadcasted_iota(jnp.int32, (LANES, tiles * LANES), 1)
     pick = jnp.where(rows == (places // LANES) * TILE + places % TILE, 1.0, 0.0).astype(jnp.bfloat16)
     spread[...] = jnp.dot(series[...], pick, preferred_element_type=f32)
-
-    weights = jnp.concatenate([bands[g].astype(jnp.bfloat16) for g in range(pairs)], axis=1)
+    fetch.wait()
+
     halves = radii * TILE // LANES
-    for j in range(tiles):
-        left = jnp.concatenate(
-            [windows[j, pl.ds(2 * g, cols)].reshape(cols * frames, LANES) for g in range(pairs)], axis=1
-        )
-        total = lax.dot_general(left, weights, (((1,), (1,)), ((), ())), preferred_element_type=f32)
-        for h in range(halves):
-            sums[j, h] = total[:, h * LANES : (h + 1) * LANES]
-
     starts = [frames - lag_list[l] for l in range(lags)]
     for j in range(tiles):
         totals = [[None] * halves for _ in range(lags)]
@@ -230,7 +262,6 @@
             for h in range(halves):
                 parts[j, l, h] = totals[l][h]
 
-    counts = jnp.sum(mask[...], axis=1, keepdims=True)
     group = lane_iota((cols, LANES)) // TILE
     for r in range(radii):
         h, rr = r // PACK, r % PACK
@@ -250,51 +281,59 @@
     radii, side = cycle_masks.shape[:2]
     lags = lag_list.shape[0]
     assert rows == LANES and frames == RMAX and side == 2 * RMAX + 1 and cols % 8 == 0 and cols >= RMAX
-    assert lax.axis_size("row") == 2 and radii * TILE % LANES == 0
-    mask = jnp.pad(cycle_masks.astype(jnp.float32), ((0, 0), (0, side % 2), (0, SPAN - side)))
-    mask = mask.reshape(radii, -1)
+    assert lax.axis_size("row") == 2 and radii % 8 == 0 and radii * TILE % LANES == 0
     groups = cols // PACK
     ext = cols + 2 * RMAX
+    tiles, halves = LANES // TILE, radii * TILE // LANES
+    pairs = (side + 1) // 2
     f32, bf16 = jnp.float32, jnp.bfloat16
     vmem = pl.BlockSpec(memory_space=pltpu.VMEM)
-    field, halo, series = pl.pallas_call(
-        functools.partial(exchange_body, frames, cols),
+    far = pl.BlockSpec(memory_space=pltpu.HBM)
+    sums, counts, series, lag_near = pl.pallas_call(
+        functools.partial(annulus_body, frames, cols, radii),
         out_shape=(
-            jax.ShapeDtypeStruct((ext + 1, frames, LANES), bf16),
-            jax.ShapeDtypeStruct((ext // PACK, frames, LANES), bf16),
+            jax.ShapeDtypeStruct((tiles, halves, cols * frames, LANES), f32),
+            jax.ShapeDtypeStruct((radii, LANES), f32),
             jax.ShapeDtypeStruct((2 * frames * cols, LANES), bf16),
+            jax.ShapeDtypeStruct((lags,), jnp.int32),
         ),
-        in_specs=[vmem],
-        out_specs=(vmem, vmem, vmem),
+        in_specs=[far, far, far],
+        out_specs=(vmem, vmem, vmem, vmem),
         scratch_shapes=[
+            pltpu.VMEM((frames * cols, LANES), f32),
+            pltpu.VMEM((side, radii, side), jnp.int32),
+            pltpu.VMEM((pairs, radii * TILE, LANES), f32),
+            pltpu.VMEM((pairs * LANES, radii * TILE), bf16),
+            pltpu.VMEM((ext + 1, frames, LANES), bf16),
+            pltpu.VMEM((ext // PACK, frames, LANES), bf16),
+            pltpu.VMEM((tiles, ext, frames, LANES), bf16),
             pltpu.VMEM((cols + 2 * REACH, frames, LANES), f32),
             pltpu.VMEM((groups, frames, LANES), f32),
             pltpu.VMEM((groups, frames, LANES), bf16),
             pltpu.VMEM((groups + 2, frames, LANES), f32),
             pltpu.VMEM((cols + 2 * REACH, frames, LANES), f32),
             pltpu.VMEM((frames * cols, LANES), f32),
+            pltpu.SemaphoreType.DMA((3,)),
             pltpu.SemaphoreType.DMA((11,)),
             pltpu.SemaphoreType.DMA((11,)),
         ],
         compiler_params=pltpu.CompilerParams(
-            collective_id=0, has_side_effects=True, vmem_limit_bytes=32 * 2**20
+            collective_id=0, has_side_effects=True, vmem_limit_bytes=VMEM_SHARE
         ),
-    )(doppler.reshape(frames * cols, LANES))
-    tiles = LANES // TILE
+    )(doppler.reshape(frames * cols, LANES), jnp.transpose(cycle_masks, (1, 0, 2)), lag_list)
     out = pl.pallas_call(
         functools.partial(correlate_body, frames, cols, radii, lags),
         out_shape=jax.ShapeDtypeStruct((radii, lags, cols, LANES), f32),
-        in_specs=[pl.BlockSpec(memory_space=pltpu.SMEM), vmem, vmem, vmem, vmem],
+        in_specs=[vmem, vmem, vmem, vmem],
         out_specs=vmem,
         scratch_shapes=[
-            pltpu.VMEM((mask.shape[1] // LANES, radii * TILE, LANES), f32),
-            pltpu.VMEM((tiles, ext, frames, LANES), bf16),
-            pltpu.VMEM((tiles, radii * TILE // LANES, cols * frames, LANES), f32),
+            pltpu.SMEM((lags,), jnp.int32),
             pltpu.VMEM((2 * frames * cols, tiles * LANES), f32),
-            pltpu.VMEM((tiles, lags, radii * TILE // LANES, cols, LANES), f32),
+            pltpu.VMEM((tiles, lags, halves, cols, LANES), f32),
+            pltpu.SemaphoreType.DMA,
         ],
-        compiler_params=pltpu.CompilerParams(vmem_limit_bytes=48 * 2**20),
-    )(lag_list, mask, field, halo, series)
+        compiler_params=pltpu.CompilerParams(vmem_limit_bytes=24 * 2**20),
+    )(lag_near, counts, series, sums)
     return out[None]
 
 

time: 19.8 us -> 19.1 us (0.965)
  other arithmetic: 0.92 us -> 0 us
  local copies, waits for them, and re-layouts: 1.62 us -> 2.49 us
  Pallas kernels: 17 us -> 16.4 us
    pallas_call x1, Pallas kernels: 5.86 us -> 2.66 us  [local(): pl.pallas_call(functools.partial(correlate_body, frames, cols, radii, lag...]
    pallas_call x1, Pallas kernels: 11.2 us -> 13.8 us  [local(): pl.pallas_call(functools.partial(annulus_body, frames, cols, radii), out_...]
    unnamed x5 -> x6, local copies, waits for them, and re-layouts: 1.51 us -> 2.49 us
    convert_element_type x1 -> x0, other arithmetic: 0.92 us -> none  [local(): cycle_masks.astype(jnp.float32)]
where the time goes in v1:
time: 19.1 us; the launch traced here: 18.9 us
  Pallas kernels  16.4 us (86%)
  local copies, waits for them, and re-layouts  2.49 us (13%)
    pallas_call x1, Pallas kernels, local(): pl.pallas_call(functools.partial(annulus_body, frames, cols, radii), out_...  13.8 us
    pallas_call x1, Pallas kernels, local(): pl.pallas_call(functools.partial(correlate_body, frames, cols, radii, lag...  2.66 us
    unnamed x6, local copies, waits for them, and re-layouts  2.49 us

profile of v1, /device:TPU:0, one launch (start us, length us, event | category | flops | bytes accessed | tf_op | source)
XLA Modules:
  0.0 18.9 jit_solution(12077187698090351207)
XLA Ops:
  0.0 0.0 copy-start
  0.0 0.9 %copy-done = f32[16,24,128]{2,1,0:T(8,128)S(1)} copy-done((f32[16,24,128]{2,1,0:T(8,128)S(1)}, f32[16,24,128]{2,1,0:T(8,128)}, u32[]{:S(2)}) %copy-start) | copy-done | bytes 196632
  0.9 0.0 copy-start.1
  0.9 0.9 %copy-done.1 = s32[8,33,33]{2,0,1:T(8,128)S(1)} copy-done((s32[8,33,33]{2,0,1:T(8,128)S(1)}, s32[8,33,33]{2,0,1:T(8,128)}, u32[]{:S(2)}) %copy-start.1) | copy-done | bytes 34872
  1.8 0.0 copy-start.2
  1.8 0.7 %copy-done.2 = s32[4]{0:T(128)S(1)} copy-done((s32[4]{0:T(128)S(1)}, s32[4]{0:T(128)}, u32[]{:S(2)}) %copy-start.2) | copy-done | bytes 40
  2.5 13.8 %shard_map.37 = (f32[4,2,384,128]{3,2,1,0:T(8,128)S(1)}, f32[8,128]{1,0:T(8,128)S(1)}, bf16[768,128]{1,0:T(8,128)(2,1)S(1)}, s32[4]{0:T(128)S(1)}) custom-call(f32[384,128]{1,0:T(8,128)S(1)} %bitcast.3, s32[33,8,33]{2,1,0:T(8,128)S(1)} %bitcast.4, s32[4]{0:T(128)S(1)} %copy-done.2), custom_call_target="tpu_custom_call" | custom-call | tf_op jit(solution)/shard_map/pallas_call | solution.py:292
  16.3 2.7 %shard_map.38 = f32[8,4,24,128]{3,2,1,0:T(8,128)} custom-call(s32[4]{0:T(128)S(1)} %get-tuple-element.9.lag_far, f32[8,128]{1,0:T(8,128)S(1)} %get-tuple-element.10.counts, bf16[768,128]{1,0:T(8,128)(2,1)S(1)} %get-tuple-element.11.series, f32[4,2,384,128]{3,2,1,0:T(8,128)S(1)} %get-tuple-element.12.sums), custom_call_target="tpu_custom_call" | custom-call | tf_op jit(solution)/shard_map/pallas_call | solution.py:324
Async XLA Ops:
  0.0 0.9 %copy-start = (f32[16,24,128]{2,1,0:T(8,128)S(1)}, f32[16,24,128]{2,1,0:T(8,128)}, u32[]{:S(2)}) copy-start(f32[16,24,128]{2,1,0:T(8,128)} %param.3) | copy-start | bytes 589828
  0.9 0.9 %copy-start.1 = (s32[8,33,33]{2,0,1:T(8,128)S(1)}, s32[8,33,33]{2,0,1:T(8,128)}, u32[]{:S(2)}) copy-start(s32[8,33,33]{2,0,1:T(8,128)} %param.4) | copy-start | bytes 104548
  1.8 0.7 %copy-start.2 = (s32[4]{0:T(128)S(1)}, s32[4]{0:T(128)}, u32[]{:S(2)}) copy-start(s32[4]{0:T(128)} %lag_far.1) | copy-start | bytes 52

commit v2 on v1

--- a/solution.py
+++ b/solution.py
@@ -15,7 +15,7 @@
 PACK = LANES // TILE
 gaussian_taps = (0.05448868, 0.24420134, 0.40261995, 0.24420134, 0.05448868)
 REACH = len(gaussian_taps) // 2
-VMEM_SHARE = 24 * 2**20
+VMEM_SHARE = 60 * 2**20
 
 
 def lane_iota(shape):
@@ -39,7 +39,7 @@
     return jnp.where((lane >= base) & (lane < base + TILE), turned, jnp.zeros_like(turned))
 
 
-def build_weights(radii, mask_in, bands, weights, counts):
+def build_weights(radii, mask_in, bands, weights, counts, early):
     side = mask_in.shape[0]
     pairs = weights.shape[0] // LANES
     bits = mask_in[...].astype(jnp.float32).reshape(side * radii, side).astype(jnp.bfloat16)
@@ -47,17 +47,24 @@
     lane = lane_iota((side, LANES))
     put = [jnp.where(lane == rows + k * SPAN, 1.0, 0.0).astype(jnp.bfloat16) for k in range(2)]
     even, odd = [jnp.dot(bits, p, preferred_element_type=jnp.float32) for p in put]
-    total = None
+    pieces = []
     for g in range(pairs):
         a = 2 * g
         piece = even[a * radii : (a + 1) * radii]
         if a + 1 < side:
             piece = piece + odd[(a + 1) * radii : (a + 2) * radii]
-        total = piece if total is None else total + piece
-        for q in range(TILE):
-            bands[g, pl.ds(q, radii, stride=TILE), :] = pltpu.roll(piece, q, 1) if q else piece
-        weights[pl.ds(g * LANES, LANES), :] = bands[g].T.astype(weights.dtype)
+        pieces.append(piece)
+    total = functools.reduce(lambda x, y: x + y, pieces)
     counts[...] = jnp.broadcast_to(jnp.sum(total, axis=1, keepdims=True), counts.shape)
+
+    def build(some):
+        for g in some:
+            for q in range(TILE):
+                bands[g, pl.ds(q, radii, stride=TILE), :] = pltpu.roll(pieces[g], q, 1) if q else pieces[g]
+            weights[pl.ds(g * LANES, LANES), :] = bands[g].T.astype(weights.dtype)
+
+    build(range(early))
+    return lambda: build(range(early, pairs))
 
 
 def build_windows(places, frames, total_cols, side, field, halo, windows):
@@ -85,13 +92,14 @@
             windows[j, i] = jnp.where(lane < SPAN, first, second).astype(windows.dtype)
 
 
-def annulus_body(frames, cols, radii, dop_far, mask_far, lag_far, sums, counts, series, lag_near, dop, mask_in, bands, weights,
-                 field, halo, windows, wide, packs, packed16, halo_in, unpacked, natural, local_sem, send, recv):
+def body(frames, cols, radii, lags, dop_far, mask_far, lag_far, out_far, sums, counts, series, lag_list, spread, parts,
+         out, dop, mask_in, bands, weights, field, halo, windows, wide, packs, packed16, halo_in, unpacked, natural,
+         local_sem, out_sem, send, recv):
     fetch_dop = pltpu.make_async_copy(dop_far, dop, local_sem.at[0])
     fetch_mask = pltpu.make_async_copy(mask_far, mask_in, local_sem.at[1])
     fetch_dop.start()
     fetch_mask.start()
-    fetch_lags = pltpu.make_async_copy(lag_far, lag_near, local_sem.at[2])
+    fetch_lags = pltpu.make_async_copy(lag_far, lag_list, local_sem.at[2])
     fetch_lags.start()
     count_s, count_t = lax.axis_size("space"), lax.axis_size("tm")
     s, t, side = lax.axis_index("space"), lax.axis_index("tm"), lax.axis_index("row")
@@ -171,13 +179,22 @@
         (copy(10, series.at[pl.ds(sent, sent)], series.at[pl.ds(0, sent)], nxt), has_nx, has_pr),
     ]
 
+    def spread_frames(start):
+        size = LANES // TILE * LANES
+        rows = lax.broadcasted_iota(jnp.int32, (LANES, size), 0)
+        places = lax.broadcasted_iota(jnp.int32, (LANES, size), 1)
+        pick = jnp.where(rows == (places // LANES) * TILE + places % TILE, 1.0, 0.0).astype(series.dtype)
+        chosen = jnp.dot(series[pl.ds(start, frames * cols)], pick, preferred_element_type=jnp.float32)
+        spread[pl.ds(start // cols, frames)] = chosen.reshape(frames, cols, size)
+
     met = lambda flag: jnp.where(flag, 1, 0).astype(jnp.int32)
     pl.semaphore_wait(barrier, 1 + 2 * met(has_lo) + 2 * met(has_hi) + met(has_pr) + met(has_nx))
     for moved, sends, _ in first:
         when(sends, moved.start)
     fetch_mask.wait()
     fetch_lags.wait()
-    build_weights(radii, mask_in, bands, weights, counts)
+    pairs = weights.shape[0] // LANES
+    finish_weights = build_weights(radii, mask_in, bands, weights, counts, pairs // 3)
     for moved, _, receives in first:
         when(receives, moved.wait_recv)
 
@@ -211,41 +228,56 @@
 
     for moved, sends, _ in second:
         when(sends, moved.start)
+    spread_frames(frames * cols)
+    finish_weights()
     for moved, sends, _ in first:
         when(sends, moved.wait_send)
     second[2][0].wait_recv()
     build_windows(range(RMAX, top - 1), frames, top + RMAX, side, field, halo, windows)
-    for moved, _, receives in second[:2] + second[3:5]:
-        when(receives, moved.wait_recv)
-    rest = list(range(RMAX)) + list(range(top - 1, top + RMAX))
-    build_windows(rest, frames, top + RMAX, side, field, halo, windows)
-
-    pairs = weights.shape[0] // LANES
-    halves = sums.shape[1]
-    for j in range(sums.shape[0]):
+
+    tiles, halves = sums.shape[:2]
+    block = 8
+    rows = block * frames
+
+    def products(start, chosen):
         left = jnp.concatenate(
-            [windows[j, pl.ds(2 * g, cols)].reshape(cols * frames, LANES) for g in range(pairs)], axis=1
+            [
+                jnp.concatenate(
+                    [windows[j, pl.ds(start + 2 * g, block)].reshape(rows, LANES) for g in chosen], axis=1
+                )
+                for j in range(tiles)
+            ],
+            axis=0,
         )
-        total = jnp.dot(left, weights[...], preferred_element_type=jnp.float32)
-        for h in range(halves):
-            sums[j, h] = total[:, h * LANES : (h + 1) * LANES]
+        right = jnp.concatenate([weights[pl.ds(g * LANES, LANES), :] for g in chosen], axis=0)
+        return jnp.dot(left, right, preferred_element_type=jnp.float32)
+
+    def inside(start, g):
+        return start + 2 * g >= RMAX and start + 2 * g + block <= top - 1
+
+    for own in (True, False):
+        for start in range(0, cols, block):
+            total = products(start, [g for g in range(pairs) if inside(start, g) == own])
+            for j in range(tiles):
+                for h in range(halves):
+                    piece = total[j * rows : (j + 1) * rows, h * LANES : (h + 1) * LANES]
+                    place = pl.ds(start * frames, rows)
+                    sums[j, h, place, :] = piece if own else sums[j, h, place, :] + piece
+        if own:
+            for moved, _, receives in second[:2] + second[3:5]:
+                when(receives, moved.wait_recv)
+            rest = list(range(RMAX)) + list(range(top - 1, top + RMAX))
+            build_windows(rest, frames, top + RMAX, side, field, halo, windows)
 
     when(has_pr, second[5][0].wait_recv)
+    spread_frames(0)
+    correlate(frames, cols, radii, lags, lag_list, counts, sums, spread, parts, out, out_far, out_sem)
     for moved, sends, _ in second:
         when(sends, moved.wait_send)
 
 
-def correlate_body(frames, cols, radii, lags, lag_far, counts, series, sums, out, lag_list, spread, parts, sem):
-    fetch = pltpu.make_async_copy(lag_far, lag_list, sem)
-    fetch.start()
+def correlate(frames, cols, radii, lags, lag_list, counts, sums, spread, parts, out, out_far, out_sem):
     tiles = LANES // TILE
-    f32 = jnp.float32
-    rows = lax.broadcasted_iota(jnp.int32, (LANES, tiles * LANES), 0)
-    places = lax.broadcasted_iota(jnp.int32, (LANES, tiles * LANES), 1)
-    pick = jnp.where(rows == (places // LANES) * TILE + places % TILE, 1.0, 0.0).astype(jnp.bfloat16)
-    spread[...] = jnp.dot(series[...], pick, preferred_element_type=f32)
-    fetch.wait()
-
     halves = radii * TILE // LANES
     starts = [frames - lag_list[l] for l in range(lags)]
     for j in range(tiles):
@@ -253,8 +285,7 @@
         for t in range(frames):
             annulus = [sums[j, h, pl.ds(t, cols, stride=frames), :] for h in range(halves)]
             for l in range(lags):
-                begin = pl.multiple_of((starts[l] + t) * cols, 8)
-                earlier = spread[pl.ds(begin, cols), pl.ds(j * LANES, LANES)]
+                earlier = spread[starts[l] + t, :, j * LANES : (j + 1) * LANES]
                 for h in range(halves):
                     term = earlier * annulus[h]
                     totals[l][h] = term if t == 0 else totals[l][h] + term
@@ -274,6 +305,9 @@
                 piece = pltpu.roll(piece, shift, 1) if shift else piece
                 whole = piece if whole is None else jnp.where(group == j, piece, whole)
             out[r, l] = whole / count
+        pltpu.make_async_copy(out.at[r], out_far.at[r], out_sem.at[r]).start()
+    for r in range(radii):
+        pltpu.make_async_copy(out.at[r], out_far.at[r], out_sem.at[r]).wait()
 
 
 def local(doppler, cycle_masks, lag_list):
@@ -289,17 +323,19 @@
     f32, bf16 = jnp.float32, jnp.bfloat16
     vmem = pl.BlockSpec(memory_space=pltpu.VMEM)
     far = pl.BlockSpec(memory_space=pltpu.HBM)
-    sums, counts, series, lag_near = pl.pallas_call(
-        functools.partial(annulus_body, frames, cols, radii),
-        out_shape=(
-            jax.ShapeDtypeStruct((tiles, halves, cols * frames, LANES), f32),
-            jax.ShapeDtypeStruct((radii, LANES), f32),
-            jax.ShapeDtypeStruct((2 * frames * cols, LANES), bf16),
-            jax.ShapeDtypeStruct((lags,), jnp.int32),
-        ),
+    out = pl.pallas_call(
+        functools.partial(body, frames, cols, radii, lags),
+        out_shape=jax.ShapeDtypeStruct((radii, lags, cols, LANES), f32),
         in_specs=[far, far, far],
-        out_specs=(vmem, vmem, vmem, vmem),
+        out_specs=far,
         scratch_shapes=[
+            pltpu.VMEM((tiles, halves, cols * frames, LANES), f32),
+            pltpu.VMEM((radii, LANES), f32),
+            pltpu.VMEM((2 * frames * cols, LANES), bf16),
+            pltpu.SMEM((lags,), jnp.int32),
+            pltpu.VMEM((2 * frames, cols, tiles * LANES), f32),
+            pltpu.VMEM((tiles, lags, halves, cols, LANES), f32),
+            pltpu.VMEM((radii, lags, cols, LANES), f32),
             pltpu.VMEM((frames * cols, LANES), f32),
             pltpu.VMEM((side, radii, side), jnp.int32),
             pltpu.VMEM((pairs, radii * TILE, LANES), f32),
@@ -314,6 +350,7 @@
             pltpu.VMEM((cols + 2 * REACH, frames, LANES), f32),
             pltpu.VMEM((frames * cols, LANES), f32),
             pltpu.SemaphoreType.DMA((3,)),
+            pltpu.SemaphoreType.DMA((radii,)),
             pltpu.SemaphoreType.DMA((11,)),
             pltpu.SemaphoreType.DMA((11,)),
         ],
@@ -321,19 +358,6 @@
             collective_id=0, has_side_effects=True, vmem_limit_bytes=VMEM_SHARE
         ),
     )(doppler.reshape(frames * cols, LANES), jnp.transpose(cycle_masks, (1, 0, 2)), lag_list)
-    out = pl.pallas_call(
-        functools.partial(correlate_body, frames, cols, radii, lags),
-        out_shape=jax.ShapeDtypeStruct((radii, lags, cols, LANES), f32),
-        in_specs=[vmem, vmem, vmem, vmem],
-        out_specs=vmem,
-        scratch_shapes=[
-            pltpu.SMEM((lags,), jnp.int32),
-            pltpu.VMEM((2 * frames * cols, tiles * LANES), f32),
-            pltpu.VMEM((tiles, lags, halves, cols, LANES), f32),
-            pltpu.SemaphoreType.DMA,
-        ],
-        compiler_params=pltpu.CompilerParams(vmem_limit_bytes=24 * 2**20),
-    )(lag_near, counts, series, sums)
     return out[None]
 
 

time: 19.1 us -> 17.5 us (0.916)
  Pallas kernels: 16.4 us -> 15.6 us
  local copies, waits for them, and re-layouts: 2.49 us -> 1.77 us
    pallas_call x2 -> x1, Pallas kernels: 16.4 us -> 15.6 us  [local(): pl.pallas_call(functools.partial(body, frames, cols, radii, lags), out_sh...]
    unnamed x6 -> x1, local copies, waits for them, and re-layouts: 2.49 us -> 1.77 us
where the time goes in v2:
time: 17.5 us; the launch traced here: 17.3 us
  Pallas kernels  15.6 us (89%)
  local copies, waits for them, and re-layouts  1.77 us (10%)
    pallas_call x1, Pallas kernels, local(): pl.pallas_call(functools.partial(body, frames, cols, radii, lags), out_sh...  15.6 us
    unnamed x1, local copies, waits for them, and re-layouts  1.77 us

profile of v2, /device:TPU:0, one launch (start us, length us, event | category | flops | bytes accessed | tf_op | source)
XLA Modules:
  0.0 17.3 jit_solution(9513896085129675159)
XLA Ops:
  0.0 15.6 %shard_map.37 = f32[8,4,24,128]{3,2,1,0:T(8,128)} custom-call(f32[384,128]{1,0:T(8,128)} %bitcast.4, s32[33,8,33]{2,1,0:T(8,128)} %bitcast.5, s32[4]{0:T(128)} %lag_far.1), custom_call_target="tpu_custom_call" | custom-call | tf_op jit(solution)/shard_map/pallas_call | solution.py:326
  15.6 1.8 %copy.5 = f32[1,8,4,24,128]{4,3,2,1,0:T(8,128)} copy(f32[1,8,4,24,128]{4,3,2,1,0:T(8,128)} %bitcast.3) | data formatting | bytes 786432

commit v3 on v2

--- a/solution.py
+++ b/solution.py
@@ -41,7 +41,7 @@
 
 def build_weights(radii, mask_in, bands, weights, counts, early):
     side = mask_in.shape[0]
-    pairs = weights.shape[0] // LANES
+    pairs = weights.shape[1] // LANES
     bits = mask_in[...].astype(jnp.float32).reshape(side * radii, side).astype(jnp.bfloat16)
     rows = lax.broadcasted_iota(jnp.int32, (side, LANES), 0)
     lane = lane_iota((side, LANES))
@@ -61,7 +61,7 @@
         for g in some:
             for q in range(TILE):
                 bands[g, pl.ds(q, radii, stride=TILE), :] = pltpu.roll(pieces[g], q, 1) if q else pieces[g]
-            weights[pl.ds(g * LANES, LANES), :] = bands[g].T.astype(weights.dtype)
+            weights[:, pl.ds(g * LANES, LANES)] = bands[g].astype(weights.dtype)
 
     build(range(early))
     return lambda: build(range(early, pairs))
@@ -92,7 +92,7 @@
             windows[j, i] = jnp.where(lane < SPAN, first, second).astype(windows.dtype)
 
 
-def body(frames, cols, radii, lags, dop_far, mask_far, lag_far, out_far, sums, counts, series, lag_list, spread, parts,
+def body(frames, cols, radii, lags, dop_far, mask_far, lag_far, out_far, counts, sums, series, lag_list, spread, parts,
          out, dop, mask_in, bands, weights, field, halo, windows, wide, packs, packed16, halo_in, unpacked, natural,
          local_sem, out_sem, send, recv):
     fetch_dop = pltpu.make_async_copy(dop_far, dop, local_sem.at[0])
@@ -193,7 +193,7 @@
         when(sends, moved.start)
     fetch_mask.wait()
     fetch_lags.wait()
-    pairs = weights.shape[0] // LANES
+    pairs = weights.shape[1] // LANES
     finish_weights = build_weights(radii, mask_in, bands, weights, counts, pairs // 3)
     for moved, _, receives in first:
         when(receives, moved.wait_recv)
@@ -249,8 +249,8 @@
             ],
             axis=0,
         )
-        right = jnp.concatenate([weights[pl.ds(g * LANES, LANES), :] for g in chosen], axis=0)
-        return jnp.dot(left, right, preferred_element_type=jnp.float32)
+        right = jnp.concatenate([weights[:, pl.ds(g * LANES, LANES)] for g in chosen], axis=1)
+        return lax.dot_general(left, right, (((1,), (1,)), ((), ())), preferred_element_type=jnp.float32)
 
     def inside(start, g):
         return start + 2 * g >= RMAX and start + 2 * g + block <= top - 1
@@ -271,12 +271,12 @@
 
     when(has_pr, second[5][0].wait_recv)
     spread_frames(0)
-    correlate(frames, cols, radii, lags, lag_list, counts, sums, spread, parts, out, out_far, out_sem)
+    correlate(frames, cols, radii, lags, lag_list, sums, spread, parts, out, out_far, out_sem)
     for moved, sends, _ in second:
         when(sends, moved.wait_send)
 
 
-def correlate(frames, cols, radii, lags, lag_list, counts, sums, spread, parts, out, out_far, out_sem):
+def correlate(frames, cols, radii, lags, lag_list, sums, spread, parts, out, out_far, out_sem):
     tiles = LANES // TILE
     halves = radii * TILE // LANES
     starts = [frames - lag_list[l] for l in range(lags)]
@@ -296,7 +296,6 @@
     group = lane_iota((cols, LANES)) // TILE
     for r in range(radii):
         h, rr = r // PACK, r % PACK
-        count = counts[r : r + 1, 0:1]
         for l in range(lags):
             whole = None
             for j in range(tiles):
@@ -304,7 +303,7 @@
                 piece = parts[j, l, h]
                 piece = pltpu.roll(piece, shift, 1) if shift else piece
                 whole = piece if whole is None else jnp.where(group == j, piece, whole)
-            out[r, l] = whole / count
+            out[r, l] = whole
         pltpu.make_async_copy(out.at[r], out_far.at[r], out_sem.at[r]).start()
     for r in range(radii):
         pltpu.make_async_copy(out.at[r], out_far.at[r], out_sem.at[r]).wait()
@@ -321,16 +320,17 @@
     tiles, halves = LANES // TILE, radii * TILE // LANES
     pairs = (side + 1) // 2
     f32, bf16 = jnp.float32, jnp.bfloat16
-    vmem = pl.BlockSpec(memory_space=pltpu.VMEM)
     far = pl.BlockSpec(memory_space=pltpu.HBM)
-    out = pl.pallas_call(
+    out, counts = pl.pallas_call(
         functools.partial(body, frames, cols, radii, lags),
-        out_shape=jax.ShapeDtypeStruct((radii, lags, cols, LANES), f32),
+        out_shape=(
+            jax.ShapeDtypeStruct((radii, lags, cols, LANES), f32),
+            jax.ShapeDtypeStruct((radii, LANES), f32),
+        ),
         in_specs=[far, far, far],
-        out_specs=far,
+        out_specs=(far, pl.BlockSpec(memory_space=pltpu.VMEM)),
         scratch_shapes=[
             pltpu.VMEM((tiles, halves, cols * frames, LANES), f32),
-            pltpu.VMEM((radii, LANES), f32),
             pltpu.VMEM((2 * frames * cols, LANES), bf16),
             pltpu.SMEM((lags,), jnp.int32),
             pltpu.VMEM((2 * frames, cols, tiles * LANES), f32),
@@ -339,7 +339,7 @@
             pltpu.VMEM((frames * cols, LANES), f32),
             pltpu.VMEM((side, radii, side), jnp.int32),
             pltpu.VMEM((pairs, radii * TILE, LANES), f32),
-            pltpu.VMEM((pairs * LANES, radii * TILE), bf16),
+            pltpu.VMEM((radii * TILE, pairs * LANES), bf16),
             pltpu.VMEM((ext + 1, frames, LANES), bf16),
             pltpu.VMEM((ext // PACK, frames, LANES), bf16),
             pltpu.VMEM((tiles, ext, frames, LANES), bf16),
@@ -358,7 +358,7 @@
             collective_id=0, has_side_effects=True, vmem_limit_bytes=VMEM_SHARE
         ),
     )(doppler.reshape(frames * cols, LANES), jnp.transpose(cycle_masks, (1, 0, 2)), lag_list)
-    return out[None]
+    return (out / counts[:, None, None, :])[None]
 
 
 def solution(mesh):

time: 17.5 us -> 17.8 us (1.017)
  other arithmetic: 0 us -> 1.78 us
  local copies, waits for them, and re-layouts: 1.77 us -> 0 us
  Pallas kernels: 15.6 us -> 15.8 us
    broadcast_in_dim x0 -> x1, other arithmetic: none -> 1.78 us  [local(): return (out / counts[:, None, None, :])[None]]
    unnamed x1 -> x0, local copies, waits for them, and re-layouts: 1.77 us -> none
    pallas_call x1, Pallas kernels: 15.6 us -> 15.8 us  [local(): pl.pallas_call(functools.partial(body, frames, cols, radii, lags), out_sh...]
where the time goes in v3:
time: 17.8 us; the launch traced here: 17.6 us
  Pallas kernels  15.8 us (89%)
  other arithmetic  1.78 us (10%)
    pallas_call x1, Pallas kernels, local(): pl.pallas_call(functools.partial(body, frames, cols, radii, lags), out_sh...  15.8 us
    broadcast_in_dim x1, other arithmetic, local(): return (out / counts[:, None, None, :])[None]  1.78 us

profile of v3, /device:TPU:0, one launch (start us, length us, event | category | flops | bytes accessed | tf_op | source)
XLA Modules:
  0.0 17.6 jit_solution(4258590699880074885)
XLA Ops:
  0.0 15.8 %shard_map.37 = (f32[8,4,24,128]{3,2,1,0:T(8,128)}, f32[8,128]{1,0:T(8,128)}) custom-call(f32[384,128]{1,0:T(8,128)} %bitcast.4, s32[33,8,33]{2,1,0:T(8,128)} %bitcast.5, s32[4]{0:T(128)} %lag_far.1), custom_call_target="tpu_custom_call" | custom-call | tf_op jit(solution)/shard_map/pallas_call | solution.py:324
  15.8 1.8 %divide_bitcast_fusion = f32[1,8,4,24,128]{4,3,2,1,0:T(8,128)} fusion(f32[8,4,24,128]{3,2,1,0:T(8,128)} %get-tuple-element.7, f32[8,128]{1,0:T(8,128)} %get-tuple-element.8), kind=kLoop, calls=%fused_computation | loop fusion | flops 98304 | bytes 790528 | tf_op jit(solution)/shard_map/broadcast_in_dim | solution.py:361

commit v4 on v2

--- a/solution.py
+++ b/solution.py
@@ -263,36 +263,40 @@
                     piece = total[j * rows : (j + 1) * rows, h * LANES : (h + 1) * LANES]
                     place = pl.ds(start * frames, rows)
                     sums[j, h, place, :] = piece if own else sums[j, h, place, :] + piece
+            if not own:
+                correlate(start, block, frames, lags, lag_list, sums, spread, parts)
         if own:
-            for moved, _, receives in second[:2] + second[3:5]:
+            for moved, _, receives in second[:2] + second[3:]:
                 when(receives, moved.wait_recv)
             rest = list(range(RMAX)) + list(range(top - 1, top + RMAX))
             build_windows(rest, frames, top + RMAX, side, field, halo, windows)
-
-    when(has_pr, second[5][0].wait_recv)
-    spread_frames(0)
-    correlate(frames, cols, radii, lags, lag_list, counts, sums, spread, parts, out, out_far, out_sem)
+            spread_frames(0)
+
+    assemble(radii, lags, counts, parts, out, out_far, out_sem)
     for moved, sends, _ in second:
         when(sends, moved.wait_send)
 
 
-def correlate(frames, cols, radii, lags, lag_list, counts, sums, spread, parts, out, out_far, out_sem):
-    tiles = LANES // TILE
-    halves = radii * TILE // LANES
+def correlate(start, block, frames, lags, lag_list, sums, spread, parts):
+    tiles, halves = sums.shape[:2]
     starts = [frames - lag_list[l] for l in range(lags)]
     for j in range(tiles):
         totals = [[None] * halves for _ in range(lags)]
         for t in range(frames):
-            annulus = [sums[j, h, pl.ds(t, cols, stride=frames), :] for h in range(halves)]
+            place = pl.ds(start * frames + t, block, stride=frames)
+            annulus = [sums[j, h, place, :] for h in range(halves)]
             for l in range(lags):
-                earlier = spread[starts[l] + t, :, j * LANES : (j + 1) * LANES]
+                earlier = spread[starts[l] + t, start : start + block, j * LANES : (j + 1) * LANES]
                 for h in range(halves):
                     term = earlier * annulus[h]
                     totals[l][h] = term if t == 0 else totals[l][h] + term
         for l in range(lags):
             for h in range(halves):
-                parts[j, l, h] = totals[l][h]
-
+                parts[j, l, h, start : start + block, :] = totals[l][h]
+
+
+def assemble(radii, lags, counts, parts, out, out_far, out_sem):
+    tiles, cols = parts.shape[0], parts.shape[3]
     group = lane_iota((cols, LANES)) // TILE
     for r in range(radii):
         h, rr = r // PACK, r % PACK

time: 17.5 us -> 16.8 us (0.960)
  Pallas kernels: 15.6 us -> 14.9 us
    pallas_call x1, Pallas kernels: 15.6 us -> 14.9 us  [local(): pl.pallas_call(functools.partial(body, frames, cols, radii, lags), out_sh...]
where the time goes in v4:
time: 16.8 us; the launch traced here: 16.6 us
  Pallas kernels  14.9 us (89%)
  local copies, waits for them, and re-layouts  1.77 us (11%)
    pallas_call x1, Pallas kernels, local(): pl.pallas_call(functools.partial(body, frames, cols, radii, lags), out_sh...  14.9 us
    unnamed x1, local copies, waits for them, and re-layouts  1.77 us

profile of v4, /device:TPU:0, one launch (start us, length us, event | category | flops | bytes accessed | tf_op | source)
XLA Modules:
  0.0 16.6 jit_solution(7729114061961342370)
XLA Ops:
  0.0 14.9 %shard_map.37 = f32[8,4,24,128]{3,2,1,0:T(8,128)} custom-call(f32[384,128]{1,0:T(8,128)} %bitcast.4, s32[33,8,33]{2,1,0:T(8,128)} %bitcast.5, s32[4]{0:T(128)} %lag_far.1), custom_call_target="tpu_custom_call" | custom-call | tf_op jit(solution)/shard_map/pallas_call | solution.py:330
  14.9 1.8 %copy.5 = f32[1,8,4,24,128]{4,3,2,1,0:T(8,128)} copy(f32[1,8,4,24,128]{4,3,2,1,0:T(8,128)} %bitcast.3) | data formatting | bytes 786432
